TPU v7x, 32 devices: a whole 2x2x4 slice. The times are simulated.
32 devices in a mesh: group: 2 (over x), ctx: 4 (over y, core), exp: 4 (over z).
Axes of the slice: x: 2, y: 2, z: 4, core: 2. Of those that a mesh axis runs over, the one named last changes fastest.
Arguments:
- queries: bfloat16 [1024, 1536], P(('group', 'ctx'), 'exp'), may hold values from -10.5 to 10.5
- keys: bfloat16 [1024, 512], P(('group', 'ctx'), 'exp'), may hold values from -4 to 4
- values: bfloat16 [1024, 512], P(('group', 'ctx'), 'exp'), may hold values from -6 to 6
- residual_in: bfloat16 [1024, 1536], P(('group', 'ctx', 'exp')), may hold values from -6 to 6
- doc_lengths: int32 [4], replicated, may hold values from 1 to 384, 1024 in all
- w_out: bfloat16 [1536, 1536], P('exp', 'group'), may hold values from -0.15625 to 0.15625
- norm_gain: float32 [1536], replicated, may hold values from 0.5 to 1.5
- router: bfloat16 [1536, 16], replicated, may hold values from -0.15625 to 0.15625
- expert_ids: int32 [1024, 6], P(('group', 'ctx', 'exp')), may hold values from 0 to 15, all different within a row; in each aligned block of 32 rows (0 to 31, 32 to 63, ...) at most 18 rows name the same one
- expert_gate_up: bfloat16 [16, 1536, 1024], P(('ctx', 'exp'), 'group'), may hold values from -0.15625 to 0.15625
- expert_down: bfloat16 [16, 1536, 512], P(('ctx', 'exp'), 'group'), may hold values from -0.25 to 0.25
- shared_gate_up: bfloat16 [1536, 2, 1024], P(None, None, 'exp'), may hold values from -0.15625 to 0.15625
- shared_down: bfloat16 [1024, 1536], P('exp'), may hold values from -0.1875 to 0.1875
Outputs:
- hidden_out: bfloat16 [1024, 1536], P(('group', 'ctx', 'exp'))
Inputs may be any that keep to these rules, and one draw needn't show every extreme that they name: `doc_lengths`: documents are packed back to back in stream order and one of them has length 384. `expert_ids`: within the 32 rows of one device along group+ctx+exp, no expert is named by more than 18 routes, a bound that some block reaches.
All inputs are finite; a program needn't handle non-finite values.
Results may differ from a plain program's by a relative error of at most 0.015.
Values may be sent and summed in bfloat16 or wider, within the bound.
A program may use at most 64 MiB of HBM per device.

v0:
```python
import math
import jax
import jax.numpy as jnp
from jax import lax
from jax.sharding import PartitionSpec as P

HEAD = 128
neg_big = -1e30


def passed_along(shard, axis, by):
    length = lax.axis_size(axis)
    pairs = [(i, i + by) for i in range(length) if 0 <= i + by < length]
    return lax.ppermute(shard, axis, pairs)


def doc_starts(positions, doc_lengths):
    order = jnp.arange(doc_lengths.shape[0], dtype=jnp.int32)
    before = (order[None, :] <= order[:, None]).astype(jnp.int32)
    doc_ends = jnp.sum(before * doc_lengths[None, :], axis=1, dtype=jnp.int32)
    passed = (doc_ends[None, :] <= positions[:, None]).astype(jnp.int32)
    return jnp.sum(passed * doc_lengths[None, :], axis=1, dtype=jnp.int32)


def attend_block(soft_state, kv_block, source, query_heads, query_pos, query_start):
    run_max, run_sum, run_acc = soft_state
    rows_dev = kv_block.shape[1]
    key_pos = source * rows_dev + jnp.arange(rows_dev, dtype=jnp.int32)
    allowed = (key_pos[None, :] <= query_pos[:, None]) & (key_pos[None, :] >= query_start[:, None])
    key_heads = kv_block[0].reshape(rows_dev, -1, HEAD)
    value_heads = kv_block[1].reshape(rows_dev, -1, HEAD)
    scores = jnp.einsum(
        "tgpd,sgd->gpts", query_heads, key_heads, preferred_element_type=jnp.float32
    ) * (1.0 / math.sqrt(HEAD))
    scores = jnp.where(allowed, scores, neg_big)
    new_max = jnp.maximum(run_max, jnp.max(scores, axis=-1))
    weights = jnp.where(allowed, jnp.exp(scores - new_max[..., None]), 0.0)
    factor = jnp.exp(run_max - new_max)
    run_sum = run_sum * factor + jnp.sum(weights, axis=-1)
    run_acc = run_acc * factor[..., None] + jnp.einsum(
        "gpts,sgd->gptd",
        weights.astype(jnp.bfloat16),
        value_heads,
        preferred_element_type=jnp.float32,
    )
    return (new_max, run_sum, run_acc)


def visit_block(soft_state, kv_block, source, query_heads, query_pos, query_start):
    rows_dev = kv_block.shape[1]
    useful = (source >= 0) & (source * rows_dev + rows_dev - 1 >= query_start[0])

    def run_block(inner_state):
        return attend_block(inner_state, kv_block, source, query_heads, query_pos, query_start)

    def keep_block(inner_state):
        return inner_state

    return lax.cond(useful, run_block, keep_block, soft_state)


def turned(shard, axis, by):
    length = lax.axis_size(axis)
    return lax.ppermute(shard, axis, [(i, (i + by) % length) for i in range(length)])


def swapped(shard):
    return lax.ppermute(shard, "group", [(0, 1), (1, 0)])


def matmul(rows, weights):
    return jnp.dot(rows, weights, preferred_element_type=jnp.float32).astype(jnp.bfloat16)


def joined(own_first, own, other):
    first = jnp.where(own_first, own, other)
    second = jnp.where(own_first, other, own)
    return jnp.concatenate([first, second], axis=-1)


def summed_from(partial, length, rows, step):
    total = partial[:rows].astype(jnp.float32)
    for by in range(1, length):
        piece = partial[by * rows : (by + 1) * rows]
        total = total + turned(piece, "exp", step * by).astype(jnp.float32)
    return total


def attend_window(kv, first_key, query_heads, query_pos, query_start):
    count = kv.shape[1]
    key_pos = first_key + jnp.arange(count, dtype=jnp.int32)
    allowed = (key_pos[None, :] <= query_pos[:, None]) & (key_pos[None, :] >= query_start[:, None])
    key_heads = kv[0].reshape(count, -1, HEAD)
    value_heads = kv[1].reshape(count, -1, HEAD)
    scores = jnp.einsum(
        "tgpd,sgd->gpts", query_heads, key_heads, preferred_element_type=jnp.float32
    ) * (1.0 / math.sqrt(HEAD))
    scores = jnp.where(allowed, scores, neg_big)
    weights = jnp.where(allowed, jnp.exp(scores - jnp.max(scores, axis=-1, keepdims=True)), 0.0)
    acc = jnp.einsum(
        "gpts,sgd->gptd",
        weights.astype(jnp.bfloat16),
        value_heads,
        preferred_element_type=jnp.float32,
    )
    return acc / jnp.sum(weights, axis=-1, keepdims=True)


def on_device(
    queries,
    keys,
    values,
    residual_in,
    doc_lengths,
    w_out,
    norm_gain,
    router,
    expert_ids,
    expert_gate_up,
    expert_down,
    shared_gate_up,
    shared_down,
):
    rows_dev = queries.shape[0]
    kv_count = keys.shape[1] // HEAD
    per_kv = queries.shape[1] // HEAD // kv_count
    block_count = lax.axis_size("group") * lax.axis_size("ctx")
    look_back = min(32, block_count // 2)
    my_block = lax.axis_index("group") * lax.axis_size("ctx") + lax.axis_index("ctx")
    query_pos = my_block * rows_dev + jnp.arange(rows_dev, dtype=jnp.int32)
    query_start = doc_starts(query_pos, doc_lengths)
    query_heads = queries.reshape(rows_dev, kv_count, per_kv, HEAD)
    init_state = (
        jnp.full((kv_count, per_kv, rows_dev), neg_big, jnp.float32),
        jnp.zeros((kv_count, per_kv, rows_dev), jnp.float32),
        jnp.zeros((kv_count, per_kv, rows_dev, HEAD), jnp.float32),
    )
    group_size = lax.axis_size("group")
    swap = group_size == 2
    kv_own = jnp.stack([keys, values])
    if look_back <= 8:
        blocks = [passed_along(kv_own, ("group", "ctx"), by) for by in range(look_back - 1, 0, -1)]
        kv_all = jnp.concatenate([*blocks, kv_own], axis=1)
    if swap:
        out_other, gate_other, down_other = (
            swapped(w_out),
            swapped(expert_gate_up),
            swapped(expert_down),
        )
        own_first = lax.axis_index("group") == 0
    if look_back <= 8:
        first_key = (my_block - (look_back - 1)) * rows_dev
        attended = attend_window(kv_all, first_key, query_heads, query_pos, query_start)
    else:
        soft_state = visit_block(init_state, kv_own, my_block, query_heads, query_pos, query_start)

        def cycle_turn(turn_idx, loop_state):
            moving, inner_state = loop_state
            moving = passed_along(moving, ("group", "ctx"), 1)
            return (
                moving,
                visit_block(
                    inner_state, moving, my_block - turn_idx, query_heads, query_pos, query_start
                ),
            )

        moving, soft_state = lax.fori_loop(1, look_back, cycle_turn, (kv_own, soft_state))
        run_max, run_sum, run_acc = soft_state
        attended = run_acc / run_sum[..., None]
    attended = jnp.transpose(attended, (2, 0, 1, 3)).reshape(rows_dev, -1).astype(jnp.bfloat16)
    exp_size = lax.axis_size("exp")
    exp_me = lax.axis_index("exp")
    tok_e = rows_dev // exp_size
    ahead = [(exp_me + by) % exp_size for by in range(exp_size)]
    rolled = jnp.concatenate(
        [lax.dynamic_slice_in_dim(attended, to * tok_e, tok_e, 0) for to in ahead], axis=0
    )
    if swap:
        partial = joined(own_first, matmul(rolled, w_out), matmul(rolled, out_other))
    else:
        partial = matmul(rolled, lax.all_gather(w_out, "group", axis=1, tiled=True))
    projected = summed_from(partial, exp_size, tok_e, 1)
    stream = (residual_in.astype(jnp.float32) + projected).astype(jnp.bfloat16)
    stream_f = stream.astype(jnp.float32)
    normed = (
        stream_f
        * lax.rsqrt(jnp.mean(stream_f * stream_f, axis=-1, keepdims=True) + 1e-05)
        * norm_gain
    ).astype(jnp.bfloat16)
    expert_count = router.shape[1]
    route_count = expert_ids.shape[1]
    logits = jnp.dot(normed, router, preferred_element_type=jnp.float32)
    chosen = expert_ids[:, :, None] == jnp.arange(expert_count, dtype=jnp.int32)[None, None, :]
    picked_logits = jnp.sum(jnp.where(chosen, logits[:, None, :], 0.0), axis=-1)
    raw_gates = jax.nn.sigmoid(picked_logits)
    gate_probs = raw_gates / jnp.sum(raw_gates, axis=-1, keepdims=True)
    all_normed = jnp.concatenate(
        [normed, *[turned(normed, "exp", by) for by in range(1, exp_size)]], axis=0
    )
    shared_pre = jnp.einsum(
        "td,dkf->tkf", all_normed, shared_gate_up, preferred_element_type=jnp.float32
    )
    shared_act = (jax.nn.silu(shared_pre[:, 0]) * shared_pre[:, 1]).astype(jnp.bfloat16)
    shared_out = summed_from(matmul(shared_act, shared_down), exp_size, tok_e, -1)
    slot_count = max(2, 3 * tok_e * route_count // (2 * expert_count))
    flat_ids = expert_ids.reshape(-1)
    order = jnp.arange(flat_ids.shape[0], dtype=jnp.int32)
    earlier = (flat_ids[None, :] == flat_ids[:, None]) & (order[None, :] < order[:, None])
    slot_of = jnp.sum(earlier.astype(jnp.int32), axis=1, dtype=jnp.int32)
    target = flat_ids * slot_count + slot_of
    placing = (
        jnp.arange(expert_count * slot_count, dtype=jnp.int32)[:, None] == target[None, :]
    ).astype(jnp.bfloat16)
    placing = jnp.sum(placing.reshape(expert_count * slot_count, tok_e, route_count), axis=2)
    model_width = normed.shape[1]
    outgoing = (
        jnp.dot(placing, normed, preferred_element_type=jnp.float32)
        .astype(jnp.bfloat16)
        .reshape(expert_count, slot_count, model_width)
    )
    if not swap:
        gate_up_full = lax.all_gather(expert_gate_up, "group", axis=1, tiled=True)
        down_full = lax.all_gather(expert_down, "group", axis=1, tiled=True)
    hidden_count = expert_down.shape[2]
    local_experts = expert_gate_up.shape[0]
    arrived = lax.all_to_all(outgoing, ("ctx", "exp"), split_axis=0, concat_axis=0, tiled=True)
    sources = arrived.shape[0] // local_experts
    grouped = arrived.reshape(sources, local_experts, arrived.shape[1], arrived.shape[2])
    if swap:
        half = model_width // 2
        mine = lax.dynamic_slice_in_dim(grouped, lax.axis_index("group") * half, half, 3)
        others = lax.dynamic_slice_in_dim(grouped, (1 - lax.axis_index("group")) * half, half, 3)
        pre_act = jnp.einsum(
            "nekd,edf->nekf", mine, expert_gate_up, preferred_element_type=jnp.float32
        ) + jnp.einsum("nekd,edf->nekf", others, gate_other, preferred_element_type=jnp.float32)
    else:
        pre_act = jnp.einsum(
            "nekd,edf->nekf", grouped, gate_up_full, preferred_element_type=jnp.float32
        )
    activated = (jax.nn.silu(pre_act[..., :hidden_count]) * pre_act[..., hidden_count:]).astype(
        jnp.bfloat16
    )

    def down(rows):
        return jnp.einsum(
            "nekf,edf->nekd", activated, rows, preferred_element_type=jnp.float32
        ).astype(jnp.bfloat16)

    if swap:
        result = joined(own_first, down(expert_down), down(down_other))
    else:
        result = down(down_full)
    returned = lax.all_to_all(
        result.reshape(arrived.shape), ("ctx", "exp"), split_axis=0, concat_axis=0, tiled=True
    )
    flat_back = returned.reshape(expert_count * slot_count, model_width)
    fetched = (
        jnp.take(flat_back, target, axis=0)
        .reshape(tok_e, route_count, model_width)
        .astype(jnp.float32)
    )
    routed = jnp.sum(gate_probs[:, :, None] * fetched, axis=1)
    return (stream_f + shared_out + routed).astype(jnp.bfloat16)


def solution(mesh):
    in_specs = (
        P(("group", "ctx"), "exp"),
        P(("group", "ctx"), "exp"),
        P(("group", "ctx"), "exp"),
        P(("group", "ctx", "exp"), None),
        P(),
        P("exp", "group"),
        P(),
        P(),
        P(("group", "ctx", "exp"), None),
        P(("ctx", "exp"), "group", None),
        P(("ctx", "exp"), "group", None),
        P(None, None, "exp"),
        P("exp", None),
    )
    out_specs = P(("group", "ctx", "exp"), None)
    return jax.shard_map(
        on_device, mesh=mesh, in_specs=in_specs, out_specs=out_specs, check_vma=False
    )
```

profile of v0, /device:TPU:0, one launch (start us, length us, event | category | flops | bytes accessed | tf_op | source)
XLA Modules:
  0.0 148.1 jit_solution(8046579092838463045)
XLA Ops:
  0.0 0.9 pad_maximum_fusion.2
  0.9 2.3 %collective-permute-start.2 = (bf16[2,128,128]{2,1,0:T(8,128)(2,1)S(1)}, bf16[2,128,128]{2,1,0:T(8,128)(2,1)S(1)}, u32[]{:S(2)}, u32[]{:S(2)}) collective-permute-start(bf16[2,128,128]{2,1,0:T(8,128)(2,1)S(1)} %pad_maximum_fusion.2), channel_id=1, source_target_pairs={{0,4},{4,8},{8,12},{12,16},{16,20},{20,24},{24,28},{1,5},{5,9},{9,... | collective-permute-start | bytes 196616 | tf_op jit(solution)/shard_map/ppermute | solution.py:14
  3.3 4.4 %collective-permute-start.1 = (bf16[2,128,128]{2,1,0:T(8,128)(2,1)S(1)}, bf16[2,128,128]{2,1,0:T(8,128)(2,1)S(1)}, u32[]{:S(2)}, u32[]{:S(2)}) collective-permute-start(bf16[2,128,128]{2,1,0:T(8,128)(2,1)S(1)} %pad_maximum_fusion.2), channel_id=1, source_target_pairs={{0,8},{4,12},{8,16},{12,20},{16,24},{20,28},{1,9},{5,13},{9,17},{1... | collective-permute-start | bytes 196616 | tf_op jit(solution)/shard_map/ppermute | solution.py:14
  7.7 4.3 %collective-permute-start = (bf16[2,128,128]{2,1,0:T(8,128)(2,1)S(1)}, bf16[2,128,128]{2,1,0:T(8,128)(2,1)S(1)}, u32[]{:S(2)}, u32[]{:S(2)}) collective-permute-start(bf16[2,128,128]{2,1,0:T(8,128)(2,1)S(1)} %pad_maximum_fusion.2), channel_id=1, source_target_pairs={{0,12},{4,16},{8,20},{12,24},{16,28},{1,13},{5,17},{9,21},{13,25},... | collective-permute-start | bytes 196616 | tf_op jit(solution)/shard_map/ppermute | solution.py:14
  15.6 1.0 copy.31
  19.3 7.4 %collective-permute-done.3 = bf16[384,768]{1,0:T(8,128)(2,1)S(1)} collective-permute-done((bf16[384,768]{1,0:T(8,128)(2,1)}, bf16[384,768]{1,0:T(8,128)(2,1)S(1)}, u32[]{:S(2)}, u32[]{:S(2)}) %collective-permute-start.3) | collective-permute-done | bytes 589856 | tf_op jit(solution)/shard_map/ppermute | solution.py:68
  27.1 3.7 %collective-permute-start.6 = (bf16[32,1536]{1,0:T(8,128)(2,1)S(1)}, bf16[32,1536]{1,0:T(8,128)(2,1)S(1)}, u32[]{:S(2)}, u32[]{:S(2)}) collective-permute-start(bf16[32,1536]{1,0:T(8,128)(2,1)S(1)} %get-tuple-element.15), channel_id=1, source_target_pairs={{0,3},{1,0},{2,1},{3,2},{4,7},{5,4},{6,5},{7,6},{8,11},{9,8},{10,9... | collective-permute-start | bytes 294920 | tf_op jit(solution)/shard_map/ppermute | solution.py:64
  30.7 1.0 collective-permute-start.4
  31.8 1.5 %collective-permute-done.6 = bf16[32,1536]{1,0:T(8,128)(2,1)S(1)} collective-permute-done((bf16[32,1536]{1,0:T(8,128)(2,1)S(1)}, bf16[32,1536]{1,0:T(8,128)(2,1)S(1)}, u32[]{:S(2)}, u32[]{:S(2)}) %collective-permute-start.6) | collective-permute-done | bytes 98336 | tf_op jit(solution)/shard_map/ppermute | solution.py:64
  33.4 5.1 %collective-permute-done.5 = bf16[32,1536]{1,0:T(8,128)(2,1)S(1)} collective-permute-done((bf16[32,1536]{1,0:T(8,128)(2,1)S(1)}, bf16[32,1536]{1,0:T(8,128)(2,1)S(1)}, u32[]{:S(2)}, u32[]{:S(2)}) %collective-permute-start.5) | collective-permute-done | bytes 98336 | tf_op jit(solution)/shard_map/ppermute | solution.py:64
  39.2 1.3 reshape.190
  40.5 4.7 %all-to-all-start = ((bf16[16,18,1536]{2,1,0:T(8,128)(2,1)}), bf16[16,18,1536]{2,1,0:T(8,128)(2,1)S(1)}, u32[]{:S(2)}, u32[]{:S(2)}) async-start(bf16[16,18,1536]{2,1,0:T(8,128)(2,1)} %reshape.190), calls=%async_computation | async-start | bytes 2359296 | tf_op jit(solution)/shard_map/all_to_all | solution.py:226
  45.2 1.8 %collective-permute-start.13 = (bf16[1,768,1024]{2,1,0:T(8,128)(2,1)}, bf16[1,768,1024]{2,1,0:T(8,128)(2,1)}, u32[]{:S(2)}, u32[]{:S(2)}) collective-permute-start(bf16[1,768,1024]{2,1,0:T(8,128)(2,1)} %param.22), channel_id=1, source_target_pairs={{0,16},{16,0},{1,17},{17,1},{2,18},{18,2},{3,19},{19,3},{4,20},{20... | collective-permute-start | bytes 4718600 | tf_op jit(solution)/shard_map/ppermute | solution.py:68
  48.0 3.7 %collective-permute-start.9 = (bf16[32,1536]{1,0:T(8,128)(2,1)S(1)}, bf16[32,1536]{1,0:T(8,128)(2,1)S(1)}, u32[]{:S(2)}, u32[]{:S(2)}) collective-permute-start(bf16[32,1536]{1,0:T(8,128)(2,1)S(1)} %fusion.34), channel_id=1, source_target_pairs={{0,3},{1,0},{2,1},{3,2},{4,7},{5,4},{6,5},{7,6},{8,11},{9,8},{10,9... | collective-permute-start | bytes 294920 | tf_op jit(solution)/shard_map/ppermute | solution.py:64
  51.7 1.1 collective-permute-start.7
  52.8 26.4 %all-to-all-done = bf16[16,18,1536]{2,1,0:T(8,128)(2,1)S(1)} async-done(((bf16[16,18,1536]{2,1,0:T(8,128)(2,1)}), bf16[16,18,1536]{2,1,0:T(8,128)(2,1)S(1)}, u32[]{:S(2)}, u32[]{:S(2)}) %all-to-all-start) | async-done | bytes 884768 | tf_op jit(solution)/shard_map/all_to_all | solution.py:226
  79.2 2.2 %fusion.2 = f32[16,18,1024]{2,1,0:T(8,128)S(1)} fusion(bf16[1,768,1024]{2,1,0:T(8,128)(2,1)} %param.22, bf16[16,18,1536]{2,1,0:T(8,128)(2,1)S(1)} %all-to-all-done, s32[]{:T(128)S(6)} %select_n.128), kind=kOutput, calls=%fused_computation.5 | convolution fusion | flops 452984832 | bytes 3342340 | tf_op jit(solution)/shard_map/nekd,edf->nekf/dot_general | solution.py:233
  81.4 1.4 collective-permute-done.13
  82.8 2.2 %add_bitcast_fusion = f32[16,1,18,1024]{3,2,0,1:T(8,128)S(1)} fusion(f32[16,18,1024]{2,1,0:T(8,128)S(1)} %fusion.2, bf16[1,768,1024]{2,1,0:T(8,128)(2,1)} %collective-permute-done.13, bf16[16,18,1536]{2,1,0:T(8,128)(2,1)S(1)} %all-to-all-done, s32[]{:T(128)S(6)} %select_n.129), kind=kOutput, calls=%fused_computation.10 | convolution fusion | flops 453279744 | bytes 4915204 | tf_op jit(solution)/shard_map/nekd,edf->nekf/dot_general | solution.py:235
  85.3 0.9 copy-done.1
  86.7 12.4 %collective-permute-done.14 = bf16[1,768,512]{2,1,0:T(8,128)(2,1)} collective-permute-done((bf16[1,768,512]{2,1,0:T(8,128)(2,1)}, bf16[1,768,512]{2,1,0:T(8,128)(2,1)}, u32[]{:S(2)}, u32[]{:S(2)}) %collective-permute-start.14) | collective-permute-done | bytes 786464 | tf_op jit(solution)/shard_map/ppermute | solution.py:68
  99.1 1.6 %select_bitcast_fusion.1 = (bf16[16,1,18,768]{3,2,0,1:T(8,128)(2,1)S(1)}, bf16[16,1,18,768]{3,2,0,1:T(8,128)(2,1)S(1)}) fusion(bf16[16,18,768]{2,1,0:T(8,128)(2,1)S(1)} %convolution_convert_fusion.3, pred[]{:T(512)S(6)} %eq.48, bf16[1,768,512]{2,1,0:T(8,128)(2,1)} %collective-permute-done.14, bf16[16,1,18,512]{3,2,0,1:T(8,128)(2,1)S(1)} %fusion.11), kind=kOutput, calls=%fused_computation.29 | convolution fusion | flops 227155968 | bytes 2408449 | tf_op jit(solution)/shard_map/nekf,edf->nekd/dot_general | solution.py:245
  100.7 1.1 maximum_bitcast_fusion
  101.8 5.9 %all-to-all-start.1 = ((bf16[16,18,1536]{2,1,0:T(8,128)(2,1)}), bf16[16,18,1536]{2,1,0:T(8,128)(2,1)}, u32[]{:S(2)}, u32[]{:S(2)}) async-start(bf16[16,18,1536]{2,1,0:T(8,128)(2,1)} %maximum_bitcast_fusion), calls=%async_computation.1 | async-start | bytes 2359296 | tf_op jit(solution)/shard_map/all_to_all | solution.py:253
  110.2 1.9 %collective-permute-start.12 = (bf16[32,1536]{1,0:T(8,128)(2,1)}, bf16[32,1536]{1,0:T(8,128)(2,1)}, u32[]{:S(2)}, u32[]{:S(2)}) collective-permute-start(bf16[32,1536]{1,0:T(8,128)(2,1)} %get-tuple-element.12), channel_id=1, source_target_pairs={{0,1},{1,2},{2,3},{3,0},{4,5},{5,6},{6,7},{7,4},{8,9},{9,10},{10,1... | collective-permute-start | bytes 294920 | tf_op jit(solution)/shard_map/ppermute | solution.py:64
  112.1 2.4 %collective-permute-start.11 = (bf16[32,1536]{1,0:T(8,128)(2,1)}, bf16[32,1536]{1,0:T(8,128)(2,1)}, u32[]{:S(2)}, u32[]{:S(2)}) collective-permute-start(bf16[32,1536]{1,0:T(8,128)(2,1)} %get-tuple-element.13), channel_id=1, source_target_pairs={{0,2},{1,3},{2,0},{3,1},{4,6},{5,7},{6,4},{7,5},{8,10},{9,11},{10,... | collective-permute-start | bytes 294920 | tf_op jit(solution)/shard_map/ppermute | solution.py:64
  114.5 1.5 collective-permute-start.10
  115.9 25.9 %all-to-all-done.1 = bf16[16,18,1536]{2,1,0:T(8,128)(2,1)} async-done(((bf16[16,18,1536]{2,1,0:T(8,128)(2,1)}), bf16[16,18,1536]{2,1,0:T(8,128)(2,1)}, u32[]{:S(2)}, u32[]{:S(2)}) %all-to-all-start.1) | async-done | bytes 884768 | tf_op jit(solution)/shard_map/all_to_all | solution.py:253
  141.8 1.5 %reshape.197 = bf16[288,1536]{1,0:T(8,128)(2,1)S(1)} reshape(bf16[16,18,1536]{2,1,0:T(8,128)(2,1)} %all-to-all-done.1) | data formatting | bytes 1769472 | tf_op jit(solution)/shard_map/reshape | solution.py:256
  143.3 1.2 gather_fusion
  144.7 1.6 %multiply_reduce_fusion = f32[32,1536]{1,0:T(8,128)S(1)} fusion(bf16[32,6,1536]{2,1,0:T(8,128)(2,1)S(1)} %gather.7, f32[32,6]{1,0:T(8,128)S(1)} %copy.36, pred[32,6]{1,0:T(8,128)(4,1)} %get-tuple-element.5), kind=kLoop, calls=%fused_computation.9 | loop fusion | flops 1130496 | bytes 787392 | tf_op jit(solution)/shard_map/reduce_sum | solution.py:262
  146.4 1.7 %fusion.36 = bf16[32,1536]{1,0:T(8,128)(2,1)} fusion(f32[32,1536]{1,0:T(8,128)S(1)} %multiply_reduce_fusion, bf16[32,1536]{1,0:T(8,128)(2,1)S(1)} %get-tuple-element.8, bf16[32,1536]{1,0:T(8,128)(2,1)} %collective-permute-done.12, bf16[32,1536]{1,0:T(8,128)(2,1)} %collective-permute-done.11, bf16[32,1536]{1,0:T(8,128)(2,1)} %collective-permute-done.10, ...), kind=kLoop, calls=%fused_computation.62 | loop fusion | flops 540672 | bytes 786432 | tf_op jit(solution)/shard_map/convert_element_type | solution.py:263
  (69 shorter events, 11.7 us)
Async XLA Ops:
  0.0 108.1 %copy-start = (bf16[1536,2,256]{2,1,0:T(2,128)(2,1)S(1)}, bf16[1536,2,256]{2,1,0:T(2,128)(2,1)}, u32[]{:S(2)}) copy-start(bf16[1536,2,256]{2,1,0:T(2,128)(2,1)} %param.24) | copy-start | bytes 4718596
  0.9 15.8 %collective-permute-start.2 = (bf16[2,128,128]{2,1,0:T(8,128)(2,1)S(1)}, bf16[2,128,128]{2,1,0:T(8,128)(2,1)S(1)}, u32[]{:S(2)}, u32[]{:S(2)}) collective-permute-start(bf16[2,128,128]{2,1,0:T(8,128)(2,1)S(1)} %pad_maximum_fusion.2), channel_id=1, source_target_pairs={{0,4},{4,8},{8,12},{12,16},{16,20},{20,24},{24,28},{1,5},{5,9},{9,... | collective-permute-start | bytes 196616 | tf_op jit(solution)/shard_map/ppermute | solution.py:14
  3.3 13.4 %collective-permute-start.1 = (bf16[2,128,128]{2,1,0:T(8,128)(2,1)S(1)}, bf16[2,128,128]{2,1,0:T(8,128)(2,1)S(1)}, u32[]{:S(2)}, u32[]{:S(2)}) collective-permute-start(bf16[2,128,128]{2,1,0:T(8,128)(2,1)S(1)} %pad_maximum_fusion.2), channel_id=1, source_target_pairs={{0,8},{4,12},{8,16},{12,20},{16,24},{20,28},{1,9},{5,13},{9,17},{1... | collective-permute-start | bytes 196616 | tf_op jit(solution)/shard_map/ppermute | solution.py:14
  7.7 9.0 %collective-permute-start = (bf16[2,128,128]{2,1,0:T(8,128)(2,1)S(1)}, bf16[2,128,128]{2,1,0:T(8,128)(2,1)S(1)}, u32[]{:S(2)}, u32[]{:S(2)}) collective-permute-start(bf16[2,128,128]{2,1,0:T(8,128)(2,1)S(1)} %pad_maximum_fusion.2), channel_id=1, source_target_pairs={{0,12},{4,16},{8,20},{12,24},{16,28},{1,13},{5,17},{9,21},{13,25},... | collective-permute-start | bytes 196616 | tf_op jit(solution)/shard_map/ppermute | solution.py:14
  12.0 14.7 %collective-permute-start.3 = (bf16[384,768]{1,0:T(8,128)(2,1)}, bf16[384,768]{1,0:T(8,128)(2,1)S(1)}, u32[]{:S(2)}, u32[]{:S(2)}) collective-permute-start(bf16[384,768]{1,0:T(8,128)(2,1)} %param.18), channel_id=1, source_target_pairs={{0,16},{16,0},{1,17},{17,1},{2,18},{18,2},{3,19},{19,3},{4,20},{20... | collective-permute-start | bytes 1769480 | tf_op jit(solution)/shard_map/ppermute | solution.py:68
  17.9 1.1 copy-start.2
  18.4 20.0 %copy-start.3 = (bf16[32,1536]{1,0:T(8,128)(2,1)S(1)}, bf16[32,1536]{1,0:T(8,128)(2,1)}, u32[]{:S(2)}) copy-start(bf16[32,1536]{1,0:T(8,128)(2,1)} %param.16) | copy-start | bytes 294916
  19.3 19.4 %copy-start.6 = (f32[1536]{0:T(1024)S(1)}, f32[1536]{0:T(1024)}, u32[]{:S(2)}) copy-start(f32[1536]{0:T(1024)} %param.19) | copy-start | bytes 18436
  27.1 6.3 %collective-permute-start.6 = (bf16[32,1536]{1,0:T(8,128)(2,1)S(1)}, bf16[32,1536]{1,0:T(8,128)(2,1)S(1)}, u32[]{:S(2)}, u32[]{:S(2)}) collective-permute-start(bf16[32,1536]{1,0:T(8,128)(2,1)S(1)} %get-tuple-element.15), channel_id=1, source_target_pairs={{0,3},{1,0},{2,1},{3,2},{4,7},{5,4},{6,5},{7,6},{8,11},{9,8},{10,9... | collective-permute-start | bytes 294920 | tf_op jit(solution)/shard_map/ppermute | solution.py:64
  30.7 7.7 %collective-permute-start.5 = (bf16[32,1536]{1,0:T(8,128)(2,1)S(1)}, bf16[32,1536]{1,0:T(8,128)(2,1)S(1)}, u32[]{:S(2)}, u32[]{:S(2)}) collective-permute-start(bf16[32,1536]{1,0:T(8,128)(2,1)S(1)} %get-tuple-element.16), channel_id=1, source_target_pairs={{0,2},{1,3},{2,0},{3,1},{4,6},{5,7},{6,4},{7,5},{8,10},{9,11},{10,... | collective-permute-start | bytes 294920 | tf_op jit(solution)/shard_map/ppermute | solution.py:64
  30.7 7.7 %collective-permute-start.4 = (bf16[32,1536]{1,0:T(8,128)(2,1)S(1)}, bf16[32,1536]{1,0:T(8,128)(2,1)S(1)}, u32[]{:S(2)}, u32[]{:S(2)}) collective-permute-start(bf16[32,1536]{1,0:T(8,128)(2,1)S(1)} %get-tuple-element.14), channel_id=1, source_target_pairs={{0,1},{1,2},{2,3},{3,0},{4,5},{5,6},{6,7},{7,4},{8,9},{9,10},{10,1... | collective-permute-start | bytes 294920 | tf_op jit(solution)/shard_map/ppermute | solution.py:64
  40.5 38.7 %all-to-all-start = ((bf16[16,18,1536]{2,1,0:T(8,128)(2,1)}), bf16[16,18,1536]{2,1,0:T(8,128)(2,1)S(1)}, u32[]{:S(2)}, u32[]{:S(2)}) async-start(bf16[16,18,1536]{2,1,0:T(8,128)(2,1)} %reshape.190), calls=%async_computation | async-start | bytes 2359296 | tf_op jit(solution)/shard_map/all_to_all | solution.py:226
  45.2 37.6 %collective-permute-start.13 = (bf16[1,768,1024]{2,1,0:T(8,128)(2,1)}, bf16[1,768,1024]{2,1,0:T(8,128)(2,1)}, u32[]{:S(2)}, u32[]{:S(2)}) collective-permute-start(bf16[1,768,1024]{2,1,0:T(8,128)(2,1)} %param.22), channel_id=1, source_target_pairs={{0,16},{16,0},{1,17},{17,1},{2,18},{18,2},{3,19},{19,3},{4,20},{20... | collective-permute-start | bytes 4718600 | tf_op jit(solution)/shard_map/ppermute | solution.py:68
  47.0 52.1 %collective-permute-start.14 = (bf16[1,768,512]{2,1,0:T(8,128)(2,1)}, bf16[1,768,512]{2,1,0:T(8,128)(2,1)}, u32[]{:S(2)}, u32[]{:S(2)}) collective-permute-start(bf16[1,768,512]{2,1,0:T(8,128)(2,1)} %param.23), channel_id=1, source_target_pairs={{0,16},{16,0},{1,17},{17,1},{2,18},{18,2},{3,19},{19,3},{4,20},{20... | collective-permute-start | bytes 2359304 | tf_op jit(solution)/shard_map/ppermute | solution.py:68
  48.0 60.1 %collective-permute-start.9 = (bf16[32,1536]{1,0:T(8,128)(2,1)S(1)}, bf16[32,1536]{1,0:T(8,128)(2,1)S(1)}, u32[]{:S(2)}, u32[]{:S(2)}) collective-permute-start(bf16[32,1536]{1,0:T(8,128)(2,1)S(1)} %fusion.34), channel_id=1, source_target_pairs={{0,3},{1,0},{2,1},{3,2},{4,7},{5,4},{6,5},{7,6},{8,11},{9,8},{10,9... | collective-permute-start | bytes 294920 | tf_op jit(solution)/shard_map/ppermute | solution.py:64
  51.7 56.4 %collective-permute-start.8 = (bf16[32,1536]{1,0:T(8,128)(2,1)S(1)}, bf16[32,1536]{1,0:T(8,128)(2,1)S(1)}, u32[]{:S(2)}, u32[]{:S(2)}) collective-permute-start(bf16[32,1536]{1,0:T(8,128)(2,1)S(1)} %fusion.34), channel_id=1, source_target_pairs={{0,2},{1,3},{2,0},{3,1},{4,6},{5,7},{6,4},{7,5},{8,10},{9,11},{10,... | collective-permute-start | bytes 294920 | tf_op jit(solution)/shard_map/ppermute | solution.py:64
  51.7 56.4 %collective-permute-start.7 = (bf16[32,1536]{1,0:T(8,128)(2,1)S(1)}, bf16[32,1536]{1,0:T(8,128)(2,1)S(1)}, u32[]{:S(2)}, u32[]{:S(2)}) collective-permute-start(bf16[32,1536]{1,0:T(8,128)(2,1)S(1)} %fusion.34), channel_id=1, source_target_pairs={{0,1},{1,2},{2,3},{3,0},{4,5},{5,6},{6,7},{7,4},{8,9},{9,10},{10,1... | collective-permute-start | bytes 294920 | tf_op jit(solution)/shard_map/ppermute | solution.py:64
  85.0 1.1 copy-start.1
  101.8 5.9 %copy-start.4 = (bf16[1536,16]{0,1:T(8,128)(2,1)S(1)}, bf16[1536,16]{0,1:T(8,128)(2,1)}, u32[]{:S(2)}) copy-start(bf16[1536,16]{0,1:T(8,128)(2,1)} %param.20) | copy-start | bytes 147460
  101.8 6.1 %copy-start.5 = (s32[32,6]{0,1:T(8,128)S(1)}, s32[32,6]{0,1:T(8,128)}, u32[]{:S(2)}) copy-start(s32[32,6]{0,1:T(8,128)} %param.21) | copy-start | bytes 2308
  101.8 40.0 %all-to-all-start.1 = ((bf16[16,18,1536]{2,1,0:T(8,128)(2,1)}), bf16[16,18,1536]{2,1,0:T(8,128)(2,1)}, u32[]{:S(2)}, u32[]{:S(2)}) async-start(bf16[16,18,1536]{2,1,0:T(8,128)(2,1)} %maximum_bitcast_fusion), calls=%async_computation.1 | async-start | bytes 2359296 | tf_op jit(solution)/shard_map/all_to_all | solution.py:253
  108.1 1.1 copy-start.7
  110.2 36.1 %collective-permute-start.12 = (bf16[32,1536]{1,0:T(8,128)(2,1)}, bf16[32,1536]{1,0:T(8,128)(2,1)}, u32[]{:S(2)}, u32[]{:S(2)}) collective-permute-start(bf16[32,1536]{1,0:T(8,128)(2,1)} %get-tuple-element.12), channel_id=1, source_target_pairs={{0,1},{1,2},{2,3},{3,0},{4,5},{5,6},{6,7},{7,4},{8,9},{9,10},{10,1... | collective-permute-start | bytes 294920 | tf_op jit(solution)/shard_map/ppermute | solution.py:64
  112.1 34.2 %collective-permute-start.11 = (bf16[32,1536]{1,0:T(8,128)(2,1)}, bf16[32,1536]{1,0:T(8,128)(2,1)}, u32[]{:S(2)}, u32[]{:S(2)}) collective-permute-start(bf16[32,1536]{1,0:T(8,128)(2,1)} %get-tuple-element.13), channel_id=1, source_target_pairs={{0,2},{1,3},{2,0},{3,1},{4,6},{5,7},{6,4},{7,5},{8,10},{9,11},{10,... | collective-permute-start | bytes 294920 | tf_op jit(solution)/shard_map/ppermute | solution.py:64
  114.5 31.9 %collective-permute-start.10 = (bf16[32,1536]{1,0:T(8,128)(2,1)}, bf16[32,1536]{1,0:T(8,128)(2,1)}, u32[]{:S(2)}, u32[]{:S(2)}) collective-permute-start(bf16[32,1536]{1,0:T(8,128)(2,1)} %get-tuple-element.11), channel_id=1, source_target_pairs={{0,3},{1,0},{2,1},{3,2},{4,7},{5,4},{6,5},{7,6},{8,11},{9,8},{10,9... | collective-permute-start | bytes 294920 | tf_op jit(solution)/shard_map/ppermute | solution.py:64
where the time goes:
time: 149 us; the launch traced here: 148 us
  waiting for transfers between devices  80.2 us (54%)
  starting transfers between devices  39 us (26%)
  other arithmetic  10.2 us (7%)
  local copies, waits for them, and re-layouts  9.35 us (6%)
  matrix products  8.89 us (6%)
    all_to_all x1, waiting for transfers between devices, on_device(): lax.all_to_all(outgoing, ('ctx', 'exp'), split_axis=0, concat_axis=0, til...  26.4 us
    all_to_all x1, waiting for transfers between devices, on_device(): lax.all_to_all(result.reshape(arrived.shape), ('ctx', 'exp'), split_axis=...  25.9 us
    ppermute x3, waiting for transfers between devices, swapped(): return lax.ppermute(shard, 'group', [(0, 1), (1, 0)])  21.3 us
    ppermute x9, starting transfers between devices, turned(): lax.ppermute(shard, axis, [(i, (i + by) % length) for i in range(length)])  15.2 us
    ppermute x3, starting transfers between devices, passed_along(): return lax.ppermute(shard, axis, pairs)  11.1 us
    ppermute x9, waiting for transfers between devices, turned(): lax.ppermute(shard, axis, [(i, (i + by) % length) for i in range(length)])  6.64 us
    all_to_all x1, starting transfers between devices, on_device(): lax.all_to_all(result.reshape(arrived.shape), ('ctx', 'exp'), split_axis=...  5.92 us
    all_to_all x1, starting transfers between devices, on_device(): lax.all_to_all(outgoing, ('ctx', 'exp'), split_axis=0, concat_axis=0, til...  4.72 us
  transfers between devices with their start and end apart: 17, of which 7 were waited for; matrix products, arithmetic and copies ran while one was open for 15% of the time, Pallas kernels for 0%

commit v1 on v0

--- a/solution.py
+++ b/solution.py
@@ -6,6 +6,28 @@
 
 HEAD = 128
 neg_big = -1e30
+
+
+def split_up(x, dim, size):
+    before, after = (x.shape[:dim], x.shape[dim + 1 :])
+    return jnp.moveaxis(x.reshape(*before, size, -1, *after), dim, 0)
+
+
+def laid_out(blocks, dim):
+    shape = list(blocks.shape[1:])
+    shape[dim] *= blocks.shape[0]
+    return jnp.moveaxis(blocks, 0, dim).reshape(shape)
+
+
+def pairwise_exchange(x, axis, split_dim, concat_dim):
+    size, index = (lax.axis_size(axis), lax.axis_index(axis))
+    blocks = split_up(x, split_dim, size)
+    outs = [blocks[index]]
+    for hop in range(1, size):
+        sent = blocks[index ^ hop]
+        outs.append(lax.ppermute(sent, axis, [(i, i ^ hop) for i in range(size)]))
+    blocks = jnp.stack(outs)[index ^ jnp.arange(size)]
+    return laid_out(blocks, concat_dim)
 
 
 def passed_along(shard, axis, by):
@@ -223,7 +245,7 @@
         down_full = lax.all_gather(expert_down, "group", axis=1, tiled=True)
     hidden_count = expert_down.shape[2]
     local_experts = expert_gate_up.shape[0]
-    arrived = lax.all_to_all(outgoing, ("ctx", "exp"), split_axis=0, concat_axis=0, tiled=True)
+    arrived = pairwise_exchange(outgoing, ("ctx", "exp"), 0, 0)
     sources = arrived.shape[0] // local_experts
     grouped = arrived.reshape(sources, local_experts, arrived.shape[1], arrived.shape[2])
     if swap:

time: 149 us -> 189 us (1.27)
  waiting for transfers between devices: 80.2 us -> 103 us
  local copies, waits for them, and re-layouts: 9.35 us -> 21 us
  starting transfers between devices: 39 us -> 42.8 us
  matrix products: 8.89 us -> 10.9 us
    ppermute x0 -> x15, waiting for transfers between devices: none -> 64.1 us  [pairwise_exchange(): outs.append(lax.ppermute(sent, axis, [(i, i ^ hop) for i in range(size)]))]
    all_to_all x1 -> x0, waiting for transfers between devices: 26.4 us -> none  [on_device(): lax.all_to_all(outgoing, ('ctx', 'exp'), split_axis=0, concat_axis=0, til...]
    ppermute x3, waiting for transfers between devices: 21.3 us -> 6.47 us  [swapped(): return lax.ppermute(shard, 'group', [(0, 1), (1, 0)])]
    ppermute x0 -> x15, starting transfers between devices: none -> 12.3 us  [pairwise_exchange(): outs.append(lax.ppermute(sent, axis, [(i, i ^ hop) for i in range(size)]))]
    unnamed x18 -> x32, local copies, waits for them, and re-layouts: 3.81 us -> 11.9 us
    all_to_all x1 -> x0, starting transfers between devices: 4.72 us -> none  [on_device(): lax.all_to_all(outgoing, ('ctx', 'exp'), split_axis=0, concat_axis=0, til...]
    another operation x0 -> x2, local copies, waits for them, and re-layouts: none -> 2.03 us  [the longest x1 1.4 us: split_up(): return jnp.moveaxis(x.reshape(*before, size, -1, *after), dim, 0)]
    gather x0 -> x1, local copies, waits for them, and re-layouts: none -> 1.89 us  [pairwise_exchange(): blocks = jnp.stack(outs)[index ^ jnp.arange(size)]]
  transfers between devices with their start and end apart: 17 -> 31, of which waited for: 7 -> 19; matrix products, arithmetic and copies ran while one was open for 15% -> 20% of each run, Pallas kernels for 0% -> 0%
where the time goes in v1:
time: 189 us; the launch traced here: 188 us
  waiting for transfers between devices  103 us (54%)
  starting transfers between devices  42.8 us (23%)
  local copies, waits for them, and re-layouts  21 us (11%)
  matrix products  10.9 us (6%)
  other arithmetic  10.2 us (5%)
    ppermute x15, waiting for transfers between devices, pairwise_exchange(): outs.append(lax.ppermute(sent, axis, [(i, i ^ hop) for i in range(size)]))  64.1 us
    all_to_all x1, waiting for transfers between devices, on_device(): lax.all_to_all(result.reshape(arrived.shape), ('ctx', 'exp'), split_axis=...  26.5 us
    ppermute x9, starting transfers between devices, turned(): lax.ppermute(shard, axis, [(i, (i + by) % length) for i in range(length)])  13.7 us
    ppermute x15, starting transfers between devices, pairwise_exchange(): outs.append(lax.ppermute(sent, axis, [(i, i ^ hop) for i in range(size)]))  12.3 us
    unnamed x32, local copies, waits for them, and re-layouts  11.9 us
    ppermute x3, starting transfers between devices, passed_along(): return lax.ppermute(shard, axis, pairs)  10 us
    ppermute x3, waiting for transfers between devices, swapped(): return lax.ppermute(shard, 'group', [(0, 1), (1, 0)])  6.47 us
    ppermute x9, waiting for transfers between devices, turned(): lax.ppermute(shard, axis, [(i, (i + by) % length) for i in range(length)])  5.96 us
  transfers between devices with their start and end apart: 31, of which 19 were waited for; matrix products, arithmetic and copies ran while one was open for 20% of the time, Pallas kernels for 0%

profile of v1, /device:TPU:0, one launch (start us, length us, event | category | flops | bytes accessed | tf_op | source)
XLA Modules:
  0.0 188.5 jit_solution(13742632474757806214)
XLA Ops:
  0.9 4.3 %collective-permute-start = (bf16[2,128,128]{2,1,0:T(8,128)(2,1)S(1)}, bf16[2,128,128]{2,1,0:T(8,128)(2,1)S(1)}, u32[]{:S(2)}, u32[]{:S(2)}) collective-permute-start(bf16[2,128,128]{2,1,0:T(8,128)(2,1)S(1)} %pad_maximum_fusion.2), channel_id=1, source_target_pairs={{0,12},{4,16},{8,20},{12,24},{16,28},{1,13},{5,17},{9,21},{13,25},... | collective-permute-start | bytes 196616 | tf_op jit(solution)/shard_map/ppermute | solution.py:36
  5.2 3.3 %collective-permute-start.1 = (bf16[2,128,128]{2,1,0:T(8,128)(2,1)S(1)}, bf16[2,128,128]{2,1,0:T(8,128)(2,1)S(1)}, u32[]{:S(2)}, u32[]{:S(2)}) collective-permute-start(bf16[2,128,128]{2,1,0:T(8,128)(2,1)S(1)} %pad_maximum_fusion.2), channel_id=1, source_target_pairs={{0,8},{4,12},{8,16},{12,20},{16,24},{20,28},{1,9},{5,13},{9,17},{1... | collective-permute-start | bytes 196616 | tf_op jit(solution)/shard_map/ppermute | solution.py:36
  8.6 2.4 %collective-permute-start.2 = (bf16[2,128,128]{2,1,0:T(8,128)(2,1)S(1)}, bf16[2,128,128]{2,1,0:T(8,128)(2,1)S(1)}, u32[]{:S(2)}, u32[]{:S(2)}) collective-permute-start(bf16[2,128,128]{2,1,0:T(8,128)(2,1)S(1)} %pad_maximum_fusion.2), channel_id=1, source_target_pairs={{0,4},{4,8},{8,12},{12,16},{16,20},{20,24},{24,28},{1,5},{5,9},{9,... | collective-permute-start | bytes 196616 | tf_op jit(solution)/shard_map/ppermute | solution.py:36
  11.0 2.0 %collective-permute-start.28 = (bf16[1,768,1024]{2,1,0:T(8,128)(2,1)}, bf16[1,768,1024]{2,1,0:T(8,128)(2,1)}, u32[]{:S(2)}, u32[]{:S(2)}) collective-permute-start(bf16[1,768,1024]{2,1,0:T(8,128)(2,1)} %param.22), channel_id=1, source_target_pairs={{0,16},{16,0},{1,17},{17,1},{2,18},{18,2},{3,19},{19,3},{4,20},{20... | collective-permute-start | bytes 4718600 | tf_op jit(solution)/shard_map/ppermute | solution.py:90
  20.7 6.5 %collective-permute-done.3 = bf16[384,768]{1,0:T(8,128)(2,1)S(1)} collective-permute-done((bf16[384,768]{1,0:T(8,128)(2,1)}, bf16[384,768]{1,0:T(8,128)(2,1)S(1)}, u32[]{:S(2)}, u32[]{:S(2)}) %collective-permute-start.3) | collective-permute-done | bytes 589856 | tf_op jit(solution)/shard_map/ppermute | solution.py:90
  29.2 2.6 %collective-permute-start.5 = (bf16[32,1536]{1,0:T(8,128)(2,1)S(1)}, bf16[32,1536]{1,0:T(8,128)(2,1)S(1)}, u32[]{:S(2)}, u32[]{:S(2)}) collective-permute-start(bf16[32,1536]{1,0:T(8,128)(2,1)S(1)} %get-tuple-element.32), channel_id=1, source_target_pairs={{0,2},{1,3},{2,0},{3,1},{4,6},{5,7},{6,4},{7,5},{8,10},{9,11},{10,... | collective-permute-start | bytes 294920 | tf_op jit(solution)/shard_map/ppermute | solution.py:86
  33.1 2.0 %collective-permute-done.4 = bf16[32,1536]{1,0:T(8,128)(2,1)S(1)} collective-permute-done((bf16[32,1536]{1,0:T(8,128)(2,1)S(1)}, bf16[32,1536]{1,0:T(8,128)(2,1)S(1)}, u32[]{:S(2)}, u32[]{:S(2)}) %collective-permute-start.4) | collective-permute-done | bytes 98336 | tf_op jit(solution)/shard_map/ppermute | solution.py:86
  35.1 3.9 %collective-permute-done.5 = bf16[32,1536]{1,0:T(8,128)(2,1)S(1)} collective-permute-done((bf16[32,1536]{1,0:T(8,128)(2,1)S(1)}, bf16[32,1536]{1,0:T(8,128)(2,1)S(1)}, u32[]{:S(2)}, u32[]{:S(2)}) %collective-permute-start.5) | collective-permute-done | bytes 98336 | tf_op jit(solution)/shard_map/ppermute | solution.py:86
  43.0 2.6 %collective-permute-start.13 = (bf16[1,18,1536]{2,1,0:T(8,128)(2,1)}, bf16[1,18,1536]{2,1,0:T(8,128)(2,1)S(1)}, u32[]{:S(2)}, u32[]{:S(2)}) collective-permute-start(bf16[1,18,1536]{2,1,0:T(8,128)(2,1)} %get-tuple-element.25), channel_id=1, source_target_pairs={{0,1},{1,0},{2,3},{3,2},{4,5},{5,4},{6,7},{7,6},{8,9},{9,8},{10,11... | collective-permute-start | bytes 165896 | tf_op jit(solution)/shard_map/ppermute | solution.py:28
  50.7 8.3 %collective-permute-done.14 = bf16[1,18,1536]{2,1,0:T(8,128)(2,1)S(1)} collective-permute-done((bf16[1,18,1536]{2,1,0:T(8,128)(2,1)}, bf16[1,18,1536]{2,1,0:T(8,128)(2,1)S(1)}, u32[]{:S(2)}, u32[]{:S(2)}) %collective-permute-start.14) | collective-permute-done | bytes 55328 | tf_op jit(solution)/shard_map/ppermute | solution.py:28
  61.4 4.0 %collective-permute-done.15 = bf16[1,18,1536]{2,1,0:T(8,128)(2,1)S(1)} collective-permute-done((bf16[1,18,1536]{2,1,0:T(8,128)(2,1)}, bf16[1,18,1536]{2,1,0:T(8,128)(2,1)S(1)}, u32[]{:S(2)}, u32[]{:S(2)}) %collective-permute-start.15) | collective-permute-done | bytes 55328 | tf_op jit(solution)/shard_map/ppermute | solution.py:28
  67.5 3.8 %collective-permute-done.17 = bf16[1,18,1536]{2,1,0:T(8,128)(2,1)S(1)} collective-permute-done((bf16[1,18,1536]{2,1,0:T(8,128)(2,1)}, bf16[1,18,1536]{2,1,0:T(8,128)(2,1)S(1)}, u32[]{:S(2)}, u32[]{:S(2)}) %collective-permute-start.17) | collective-permute-done | bytes 55328 | tf_op jit(solution)/shard_map/ppermute | solution.py:28
  72.4 5.5 %collective-permute-done.18 = bf16[1,18,1536]{2,1,0:T(8,128)(2,1)S(1)} collective-permute-done((bf16[1,18,1536]{2,1,0:T(8,128)(2,1)}, bf16[1,18,1536]{2,1,0:T(8,128)(2,1)S(1)}, u32[]{:S(2)}, u32[]{:S(2)}) %collective-permute-start.18) | collective-permute-done | bytes 55328 | tf_op jit(solution)/shard_map/ppermute | solution.py:28
  80.2 4.0 %collective-permute-done.19 = bf16[1,18,1536]{2,1,0:T(8,128)(2,1)S(1)} collective-permute-done((bf16[1,18,1536]{2,1,0:T(8,128)(2,1)}, bf16[1,18,1536]{2,1,0:T(8,128)(2,1)S(1)}, u32[]{:S(2)}, u32[]{:S(2)}) %collective-permute-start.19) | collective-permute-done | bytes 55328 | tf_op jit(solution)/shard_map/ppermute | solution.py:28
  84.9 3.9 %collective-permute-done.20 = bf16[1,18,1536]{2,1,0:T(8,128)(2,1)S(1)} collective-permute-done((bf16[1,18,1536]{2,1,0:T(8,128)(2,1)}, bf16[1,18,1536]{2,1,0:T(8,128)(2,1)S(1)}, u32[]{:S(2)}, u32[]{:S(2)}) %collective-permute-start.20) | collective-permute-done | bytes 55328 | tf_op jit(solution)/shard_map/ppermute | solution.py:28
  89.4 4.6 %collective-permute-done.21 = bf16[1,18,1536]{2,1,0:T(8,128)(2,1)S(1)} collective-permute-done((bf16[1,18,1536]{2,1,0:T(8,128)(2,1)S(1)}, bf16[1,18,1536]{2,1,0:T(8,128)(2,1)S(1)}, u32[]{:S(2)}, u32[]{:S(2)}) %collective-permute-start.21) | collective-permute-done | bytes 55328 | tf_op jit(solution)/shard_map/ppermute | solution.py:28
  95.1 5.8 %collective-permute-done.22 = bf16[1,18,1536]{2,1,0:T(8,128)(2,1)S(1)} collective-permute-done((bf16[1,18,1536]{2,1,0:T(8,128)(2,1)S(1)}, bf16[1,18,1536]{2,1,0:T(8,128)(2,1)S(1)}, u32[]{:S(2)}, u32[]{:S(2)}) %collective-permute-start.22) | collective-permute-done | bytes 55328 | tf_op jit(solution)/shard_map/ppermute | solution.py:28
  100.9 1.7 collective-permute-start.23
  103.3 4.7 %collective-permute-done.23 = bf16[1,18,1536]{2,1,0:T(8,128)(2,1)S(1)} collective-permute-done((bf16[1,18,1536]{2,1,0:T(8,128)(2,1)S(1)}, bf16[1,18,1536]{2,1,0:T(8,128)(2,1)S(1)}, u32[]{:S(2)}, u32[]{:S(2)}) %collective-permute-start.23) | collective-permute-done | bytes 55328 | tf_op jit(solution)/shard_map/ppermute | solution.py:28
  108.6 3.1 %collective-permute-done.24 = bf16[1,18,1536]{2,1,0:T(8,128)(2,1)S(1)} collective-permute-done((bf16[1,18,1536]{2,1,0:T(8,128)(2,1)S(1)}, bf16[1,18,1536]{2,1,0:T(8,128)(2,1)S(1)}, u32[]{:S(2)}, u32[]{:S(2)}) %collective-permute-start.24) | collective-permute-done | bytes 55328 | tf_op jit(solution)/shard_map/ppermute | solution.py:28
  112.4 4.0 %collective-permute-done.25 = bf16[1,18,1536]{2,1,0:T(8,128)(2,1)S(1)} collective-permute-done((bf16[1,18,1536]{2,1,0:T(8,128)(2,1)S(1)}, bf16[1,18,1536]{2,1,0:T(8,128)(2,1)S(1)}, u32[]{:S(2)}, u32[]{:S(2)}) %collective-permute-start.25) | collective-permute-done | bytes 55328 | tf_op jit(solution)/shard_map/ppermute | solution.py:28
  117.5 5.8 %collective-permute-done.26 = bf16[1,18,1536]{2,1,0:T(8,128)(2,1)S(1)} collective-permute-done((bf16[1,18,1536]{2,1,0:T(8,128)(2,1)S(1)}, bf16[1,18,1536]{2,1,0:T(8,128)(2,1)S(1)}, u32[]{:S(2)}, u32[]{:S(2)}) %collective-permute-start.26) | collective-permute-done | bytes 55328 | tf_op jit(solution)/shard_map/ppermute | solution.py:28
  123.3 1.7 collective-permute-start.27
  125.7 4.8 %collective-permute-done.27 = bf16[1,18,1536]{2,1,0:T(8,128)(2,1)S(1)} collective-permute-done((bf16[1,18,1536]{2,1,0:T(8,128)(2,1)S(1)}, bf16[1,18,1536]{2,1,0:T(8,128)(2,1)S(1)}, u32[]{:S(2)}, u32[]{:S(2)}) %collective-permute-start.27) | collective-permute-done | bytes 55328 | tf_op jit(solution)/shard_map/ppermute | solution.py:28
  130.5 1.8 collective-permute-start.9
  133.0 1.9 %gather_fusion = bf16[16,18,1536]{2,1,0:T(8,128)(2,1)S(1)} fusion(bf16[16,18,1536]{2,1,0:T(8,128)(2,1)} %bitcast.166, s32[1024]{0:T(1024)S(1)} %pad_clamp_fusion.1), kind=kCustom, calls=%fused_computation | custom fusion | bytes 1769536 | tf_op jit(solution)/shard_map/gather | solution.py:29
  134.9 2.2 %fusion.2 = f32[16,18,1024]{2,1,0:T(8,128)S(1)} fusion(bf16[1,768,1024]{2,1,0:T(8,128)(2,1)} %param.22, bf16[16,18,1536]{2,1,0:T(8,128)(2,1)S(1)} %gather_fusion, s32[]{:T(128)S(6)} %select_n.203), kind=kOutput, calls=%fused_computation.6 | convolution fusion | flops 452984832 | bytes 3342340 | tf_op jit(solution)/shard_map/nekd,edf->nekf/dot_general | solution.py:255
  137.1 2.2 %add_bitcast_fusion = f32[16,1,18,1024]{3,2,0,1:T(8,128)S(1)} fusion(f32[16,18,1024]{2,1,0:T(8,128)S(1)} %fusion.2, bf16[1,768,1024]{2,1,0:T(8,128)(2,1)} %collective-permute-done.28, bf16[16,18,1536]{2,1,0:T(8,128)(2,1)S(1)} %gather_fusion, s32[]{:T(128)S(6)} %select_n.204), kind=kOutput, calls=%fused_computation.11 | convolution fusion | flops 453279744 | bytes 4915204 | tf_op jit(solution)/shard_map/nekd,edf->nekf/dot_general | solution.py:257
  143.7 4.5 %all-to-all-start = ((bf16[16,18,1536]{2,1,0:T(8,128)(2,1)}), bf16[16,18,1536]{2,1,0:T(8,128)(2,1)}, u32[]{:S(2)}, u32[]{:S(2)}) async-start(bf16[16,18,1536]{2,1,0:T(8,128)(2,1)} %maximum_bitcast_fusion), calls=%async_computation | async-start | bytes 2359296 | tf_op jit(solution)/shard_map/all_to_all | solution.py:275
  151.0 3.6 %collective-permute-start.10 = (bf16[32,1536]{1,0:T(8,128)(2,1)}, bf16[32,1536]{1,0:T(8,128)(2,1)}, u32[]{:S(2)}, u32[]{:S(2)}) collective-permute-start(bf16[32,1536]{1,0:T(8,128)(2,1)} %get-tuple-element.27), channel_id=1, source_target_pairs={{0,3},{1,0},{2,1},{3,2},{4,7},{5,4},{6,5},{7,6},{8,11},{9,8},{10,9... | collective-permute-start | bytes 294920 | tf_op jit(solution)/shard_map/ppermute | solution.py:86
  155.7 26.5 %all-to-all-done = bf16[16,18,1536]{2,1,0:T(8,128)(2,1)} async-done(((bf16[16,18,1536]{2,1,0:T(8,128)(2,1)}), bf16[16,18,1536]{2,1,0:T(8,128)(2,1)}, u32[]{:S(2)}, u32[]{:S(2)}) %all-to-all-start) | async-done | bytes 884768 | tf_op jit(solution)/shard_map/all_to_all | solution.py:275
  186.8 1.7 fusion.36
  (116 shorter events, 47.8 us)
Async XLA Ops:
  0.0 148.6 %copy-start = (bf16[1536,2,256]{2,1,0:T(2,128)(2,1)S(1)}, bf16[1536,2,256]{2,1,0:T(2,128)(2,1)}, u32[]{:S(2)}) copy-start(bf16[1536,2,256]{2,1,0:T(2,128)(2,1)} %param.24) | copy-start | bytes 4718596
  0.9 17.0 %collective-permute-start = (bf16[2,128,128]{2,1,0:T(8,128)(2,1)S(1)}, bf16[2,128,128]{2,1,0:T(8,128)(2,1)S(1)}, u32[]{:S(2)}, u32[]{:S(2)}) collective-permute-start(bf16[2,128,128]{2,1,0:T(8,128)(2,1)S(1)} %pad_maximum_fusion.2), channel_id=1, source_target_pairs={{0,12},{4,16},{8,20},{12,24},{16,28},{1,13},{5,17},{9,21},{13,25},... | collective-permute-start | bytes 196616 | tf_op jit(solution)/shard_map/ppermute | solution.py:36
  5.2 12.9 %collective-permute-start.1 = (bf16[2,128,128]{2,1,0:T(8,128)(2,1)S(1)}, bf16[2,128,128]{2,1,0:T(8,128)(2,1)S(1)}, u32[]{:S(2)}, u32[]{:S(2)}) collective-permute-start(bf16[2,128,128]{2,1,0:T(8,128)(2,1)S(1)} %pad_maximum_fusion.2), channel_id=1, source_target_pairs={{0,8},{4,12},{8,16},{12,20},{16,24},{20,28},{1,9},{5,13},{9,17},{1... | collective-permute-start | bytes 196616 | tf_op jit(solution)/shard_map/ppermute | solution.py:36
  8.6 9.5 %collective-permute-start.2 = (bf16[2,128,128]{2,1,0:T(8,128)(2,1)S(1)}, bf16[2,128,128]{2,1,0:T(8,128)(2,1)S(1)}, u32[]{:S(2)}, u32[]{:S(2)}) collective-permute-start(bf16[2,128,128]{2,1,0:T(8,128)(2,1)S(1)} %pad_maximum_fusion.2), channel_id=1, source_target_pairs={{0,4},{4,8},{8,12},{12,16},{16,20},{20,24},{24,28},{1,5},{5,9},{9,... | collective-permute-start | bytes 196616 | tf_op jit(solution)/shard_map/ppermute | solution.py:36
  10.9 16.3 %collective-permute-start.3 = (bf16[384,768]{1,0:T(8,128)(2,1)}, bf16[384,768]{1,0:T(8,128)(2,1)S(1)}, u32[]{:S(2)}, u32[]{:S(2)}) collective-permute-start(bf16[384,768]{1,0:T(8,128)(2,1)} %param.18), channel_id=1, source_target_pairs={{0,16},{16,0},{1,17},{17,1},{2,18},{18,2},{3,19},{19,3},{4,20},{20... | collective-permute-start | bytes 1769480 | tf_op jit(solution)/shard_map/ppermute | solution.py:90
  11.0 126.1 %collective-permute-start.28 = (bf16[1,768,1024]{2,1,0:T(8,128)(2,1)}, bf16[1,768,1024]{2,1,0:T(8,128)(2,1)}, u32[]{:S(2)}, u32[]{:S(2)}) collective-permute-start(bf16[1,768,1024]{2,1,0:T(8,128)(2,1)} %param.22), channel_id=1, source_target_pairs={{0,16},{16,0},{1,17},{17,1},{2,18},{18,2},{3,19},{19,3},{4,20},{20... | collective-permute-start | bytes 4718600 | tf_op jit(solution)/shard_map/ppermute | solution.py:90
  18.0 123.0 %collective-permute-start.29 = (bf16[1,768,512]{2,1,0:T(8,128)(2,1)}, bf16[1,768,512]{2,1,0:T(8,128)(2,1)}, u32[]{:S(2)}, u32[]{:S(2)}) collective-permute-start(bf16[1,768,512]{2,1,0:T(8,128)(2,1)} %param.23), channel_id=1, source_target_pairs={{0,16},{16,0},{1,17},{17,1},{2,18},{18,2},{3,19},{19,3},{4,20},{20... | collective-permute-start | bytes 2359304 | tf_op jit(solution)/shard_map/ppermute | solution.py:90
  27.5 7.6 %collective-permute-start.4 = (bf16[32,1536]{1,0:T(8,128)(2,1)S(1)}, bf16[32,1536]{1,0:T(8,128)(2,1)S(1)}, u32[]{:S(2)}, u32[]{:S(2)}) collective-permute-start(bf16[32,1536]{1,0:T(8,128)(2,1)S(1)} %get-tuple-element.30), channel_id=1, source_target_pairs={{0,1},{1,2},{2,3},{3,0},{4,5},{5,6},{6,7},{7,4},{8,9},{9,10},{10,1... | collective-permute-start | bytes 294920 | tf_op jit(solution)/shard_map/ppermute | solution.py:86
  29.2 9.9 %collective-permute-start.5 = (bf16[32,1536]{1,0:T(8,128)(2,1)S(1)}, bf16[32,1536]{1,0:T(8,128)(2,1)S(1)}, u32[]{:S(2)}, u32[]{:S(2)}) collective-permute-start(bf16[32,1536]{1,0:T(8,128)(2,1)S(1)} %get-tuple-element.32), channel_id=1, source_target_pairs={{0,2},{1,3},{2,0},{3,1},{4,6},{5,7},{6,4},{7,5},{8,10},{9,11},{10,... | collective-permute-start | bytes 294920 | tf_op jit(solution)/shard_map/ppermute | solution.py:86
  31.8 7.3 %collective-permute-start.6 = (bf16[32,1536]{1,0:T(8,128)(2,1)S(1)}, bf16[32,1536]{1,0:T(8,128)(2,1)S(1)}, u32[]{:S(2)}, u32[]{:S(2)}) collective-permute-start(bf16[32,1536]{1,0:T(8,128)(2,1)S(1)} %get-tuple-element.31), channel_id=1, source_target_pairs={{0,3},{1,0},{2,1},{3,2},{4,7},{5,4},{6,5},{7,6},{8,11},{9,8},{10,9... | collective-permute-start | bytes 294920 | tf_op jit(solution)/shard_map/ppermute | solution.py:86
  43.0 5.6 %collective-permute-start.13 = (bf16[1,18,1536]{2,1,0:T(8,128)(2,1)}, bf16[1,18,1536]{2,1,0:T(8,128)(2,1)S(1)}, u32[]{:S(2)}, u32[]{:S(2)}) collective-permute-start(bf16[1,18,1536]{2,1,0:T(8,128)(2,1)} %get-tuple-element.25), channel_id=1, source_target_pairs={{0,1},{1,0},{2,3},{3,2},{4,5},{5,4},{6,7},{7,6},{8,9},{9,8},{10,11... | collective-permute-start | bytes 165896 | tf_op jit(solution)/shard_map/ppermute | solution.py:28
  46.2 102.4 %collective-permute-start.7 = (bf16[32,1536]{1,0:T(8,128)(2,1)S(1)}, bf16[32,1536]{1,0:T(8,128)(2,1)}, u32[]{:S(2)}, u32[]{:S(2)}) collective-permute-start(bf16[32,1536]{1,0:T(8,128)(2,1)S(1)} %fusion.34), channel_id=1, source_target_pairs={{0,1},{1,2},{2,3},{3,0},{4,5},{5,6},{6,7},{7,4},{8,9},{9,10},{10,1... | collective-permute-start | bytes 294920 | tf_op jit(solution)/shard_map/ppermute | solution.py:86
  46.2 102.4 %collective-permute-start.8 = (bf16[32,1536]{1,0:T(8,128)(2,1)S(1)}, bf16[32,1536]{1,0:T(8,128)(2,1)}, u32[]{:S(2)}, u32[]{:S(2)}) collective-permute-start(bf16[32,1536]{1,0:T(8,128)(2,1)S(1)} %fusion.34), channel_id=1, source_target_pairs={{0,2},{1,3},{2,0},{3,1},{4,6},{5,7},{6,4},{7,5},{8,10},{9,11},{10,... | collective-permute-start | bytes 294920 | tf_op jit(solution)/shard_map/ppermute | solution.py:86
  48.5 10.5 %collective-permute-start.14 = (bf16[1,18,1536]{2,1,0:T(8,128)(2,1)}, bf16[1,18,1536]{2,1,0:T(8,128)(2,1)S(1)}, u32[]{:S(2)}, u32[]{:S(2)}) collective-permute-start(bf16[1,18,1536]{2,1,0:T(8,128)(2,1)} %get-tuple-element.24), channel_id=1, source_target_pairs={{0,2},{1,3},{2,0},{3,1},{4,6},{5,7},{6,4},{7,5},{8,10},{9,11},{10,... | collective-permute-start | bytes 165896 | tf_op jit(solution)/shard_map/ppermute | solution.py:28
  59.1 6.4 %collective-permute-start.15 = (bf16[1,18,1536]{2,1,0:T(8,128)(2,1)}, bf16[1,18,1536]{2,1,0:T(8,128)(2,1)S(1)}, u32[]{:S(2)}, u32[]{:S(2)}) collective-permute-start(bf16[1,18,1536]{2,1,0:T(8,128)(2,1)} %get-tuple-element.23), channel_id=1, source_target_pairs={{0,3},{1,2},{2,1},{3,0},{4,7},{5,6},{6,5},{7,4},{8,11},{9,10},{10,... | collective-permute-start | bytes 165896 | tf_op jit(solution)/shard_map/ppermute | solution.py:28
  65.4 1.5 collective-permute-start.16
  66.9 4.4 %collective-permute-start.17 = (bf16[1,18,1536]{2,1,0:T(8,128)(2,1)}, bf16[1,18,1536]{2,1,0:T(8,128)(2,1)S(1)}, u32[]{:S(2)}, u32[]{:S(2)}) collective-permute-start(bf16[1,18,1536]{2,1,0:T(8,128)(2,1)} %get-tuple-element.21), channel_id=1, source_target_pairs={{0,5},{1,4},{2,7},{3,6},{4,1},{5,0},{6,3},{7,2},{8,13},{9,12},{10,... | collective-permute-start | bytes 165896 | tf_op jit(solution)/shard_map/ppermute | solution.py:28
  71.3 6.6 %collective-permute-start.18 = (bf16[1,18,1536]{2,1,0:T(8,128)(2,1)}, bf16[1,18,1536]{2,1,0:T(8,128)(2,1)S(1)}, u32[]{:S(2)}, u32[]{:S(2)}) collective-permute-start(bf16[1,18,1536]{2,1,0:T(8,128)(2,1)} %get-tuple-element.20), channel_id=1, source_target_pairs={{0,6},{1,7},{2,4},{3,5},{4,2},{5,3},{6,0},{7,1},{8,14},{9,15},{10,... | collective-permute-start | bytes 165896 | tf_op jit(solution)/shard_map/ppermute | solution.py:28
  77.9 6.3 %collective-permute-start.19 = (bf16[1,18,1536]{2,1,0:T(8,128)(2,1)}, bf16[1,18,1536]{2,1,0:T(8,128)(2,1)S(1)}, u32[]{:S(2)}, u32[]{:S(2)}) collective-permute-start(bf16[1,18,1536]{2,1,0:T(8,128)(2,1)} %get-tuple-element.19), channel_id=1, source_target_pairs={{0,7},{1,6},{2,5},{3,4},{4,3},{5,2},{6,1},{7,0},{8,15},{9,14},{10,... | collective-permute-start | bytes 165896 | tf_op jit(solution)/shard_map/ppermute | solution.py:28
  84.2 4.6 %collective-permute-start.20 = (bf16[1,18,1536]{2,1,0:T(8,128)(2,1)}, bf16[1,18,1536]{2,1,0:T(8,128)(2,1)S(1)}, u32[]{:S(2)}, u32[]{:S(2)}) collective-permute-start(bf16[1,18,1536]{2,1,0:T(8,128)(2,1)} %get-tuple-element.18), channel_id=1, source_target_pairs={{0,8},{1,9},{2,10},{3,11},{4,12},{5,13},{6,14},{7,15},{8,0},{9,1},... | collective-permute-start | bytes 165896 | tf_op jit(solution)/shard_map/ppermute | solution.py:28
  88.8 5.3 %collective-permute-start.21 = (bf16[1,18,1536]{2,1,0:T(8,128)(2,1)S(1)}, bf16[1,18,1536]{2,1,0:T(8,128)(2,1)S(1)}, u32[]{:S(2)}, u32[]{:S(2)}) collective-permute-start(bf16[1,18,1536]{2,1,0:T(8,128)(2,1)S(1)} %get-tuple-element.17), channel_id=1, source_target_pairs={{0,9},{1,8},{2,11},{3,10},{4,13},{5,12},{6,15},{7,14},{8,1},{9,0},... | collective-permute-start | bytes 165896 | tf_op jit(solution)/shard_map/ppermute | solution.py:28
  94.0 6.9 %collective-permute-start.22 = (bf16[1,18,1536]{2,1,0:T(8,128)(2,1)S(1)}, bf16[1,18,1536]{2,1,0:T(8,128)(2,1)S(1)}, u32[]{:S(2)}, u32[]{:S(2)}) collective-permute-start(bf16[1,18,1536]{2,1,0:T(8,128)(2,1)S(1)} %get-tuple-element.16), channel_id=1, source_target_pairs={{0,10},{1,11},{2,8},{3,9},{4,14},{5,15},{6,12},{7,13},{8,2},{9,3},... | collective-permute-start | bytes 165896 | tf_op jit(solution)/shard_map/ppermute | solution.py:28
  100.9 7.0 %collective-permute-start.23 = (bf16[1,18,1536]{2,1,0:T(8,128)(2,1)S(1)}, bf16[1,18,1536]{2,1,0:T(8,128)(2,1)S(1)}, u32[]{:S(2)}, u32[]{:S(2)}) collective-permute-start(bf16[1,18,1536]{2,1,0:T(8,128)(2,1)S(1)} %get-tuple-element.15), channel_id=1, source_target_pairs={{0,11},{1,10},{2,9},{3,8},{4,15},{5,14},{6,13},{7,12},{8,3},{9,2},... | collective-permute-start | bytes 165896 | tf_op jit(solution)/shard_map/ppermute | solution.py:28
  108.0 3.8 %collective-permute-start.24 = (bf16[1,18,1536]{2,1,0:T(8,128)(2,1)S(1)}, bf16[1,18,1536]{2,1,0:T(8,128)(2,1)S(1)}, u32[]{:S(2)}, u32[]{:S(2)}) collective-permute-start(bf16[1,18,1536]{2,1,0:T(8,128)(2,1)S(1)} %get-tuple-element.14), channel_id=1, source_target_pairs={{0,12},{1,13},{2,14},{3,15},{4,8},{5,9},{6,10},{7,11},{8,4},{9,5},... | collective-permute-start | bytes 165896 | tf_op jit(solution)/shard_map/ppermute | solution.py:28
  111.8 4.7 %collective-permute-start.25 = (bf16[1,18,1536]{2,1,0:T(8,128)(2,1)S(1)}, bf16[1,18,1536]{2,1,0:T(8,128)(2,1)S(1)}, u32[]{:S(2)}, u32[]{:S(2)}) collective-permute-start(bf16[1,18,1536]{2,1,0:T(8,128)(2,1)S(1)} %get-tuple-element.13), channel_id=1, source_target_pairs={{0,13},{1,12},{2,15},{3,14},{4,9},{5,8},{6,11},{7,10},{8,5},{9,4},... | collective-permute-start | bytes 165896 | tf_op jit(solution)/shard_map/ppermute | solution.py:28
  116.4 6.9 %collective-permute-start.26 = (bf16[1,18,1536]{2,1,0:T(8,128)(2,1)S(1)}, bf16[1,18,1536]{2,1,0:T(8,128)(2,1)S(1)}, u32[]{:S(2)}, u32[]{:S(2)}) collective-permute-start(bf16[1,18,1536]{2,1,0:T(8,128)(2,1)S(1)} %get-tuple-element.12), channel_id=1, source_target_pairs={{0,14},{1,15},{2,12},{3,13},{4,10},{5,11},{6,8},{7,9},{8,6},{9,7},... | collective-permute-start | bytes 165896 | tf_op jit(solution)/shard_map/ppermute | solution.py:28
  123.3 7.2 %collective-permute-start.27 = (bf16[1,18,1536]{2,1,0:T(8,128)(2,1)S(1)}, bf16[1,18,1536]{2,1,0:T(8,128)(2,1)S(1)}, u32[]{:S(2)}, u32[]{:S(2)}) collective-permute-start(bf16[1,18,1536]{2,1,0:T(8,128)(2,1)S(1)} %get-tuple-element.11), channel_id=1, source_target_pairs={{0,15},{1,14},{2,13},{3,12},{4,11},{5,10},{6,9},{7,8},{8,7},{9,6},... | collective-permute-start | bytes 165896 | tf_op jit(solution)/shard_map/ppermute | solution.py:28
  130.5 18.1 %collective-permute-start.9 = (bf16[32,1536]{1,0:T(8,128)(2,1)S(1)}, bf16[32,1536]{1,0:T(8,128)(2,1)S(1)}, u32[]{:S(2)}, u32[]{:S(2)}) collective-permute-start(bf16[32,1536]{1,0:T(8,128)(2,1)S(1)} %fusion.34), channel_id=1, source_target_pairs={{0,3},{1,0},{2,1},{3,2},{4,7},{5,4},{6,5},{7,6},{8,11},{9,8},{10,9... | collective-permute-start | bytes 294920 | tf_op jit(solution)/shard_map/ppermute | solution.py:86
  143.7 38.5 %all-to-all-start = ((bf16[16,18,1536]{2,1,0:T(8,128)(2,1)}), bf16[16,18,1536]{2,1,0:T(8,128)(2,1)}, u32[]{:S(2)}, u32[]{:S(2)}) async-start(bf16[16,18,1536]{2,1,0:T(8,128)(2,1)} %maximum_bitcast_fusion), calls=%async_computation | async-start | bytes 2359296 | tf_op jit(solution)/shard_map/all_to_all | solution.py:275
  151.0 35.7 %collective-permute-start.10 = (bf16[32,1536]{1,0:T(8,128)(2,1)}, bf16[32,1536]{1,0:T(8,128)(2,1)}, u32[]{:S(2)}, u32[]{:S(2)}) collective-permute-start(bf16[32,1536]{1,0:T(8,128)(2,1)} %get-tuple-element.27), channel_id=1, source_target_pairs={{0,3},{1,0},{2,1},{3,2},{4,7},{5,4},{6,5},{7,6},{8,11},{9,8},{10,9... | collective-permute-start | bytes 294920 | tf_op jit(solution)/shard_map/ppermute | solution.py:86
  154.6 32.2 %collective-permute-start.11 = (bf16[32,1536]{1,0:T(8,128)(2,1)}, bf16[32,1536]{1,0:T(8,128)(2,1)}, u32[]{:S(2)}, u32[]{:S(2)}) collective-permute-start(bf16[32,1536]{1,0:T(8,128)(2,1)} %get-tuple-element.29), channel_id=1, source_target_pairs={{0,2},{1,3},{2,0},{3,1},{4,6},{5,7},{6,4},{7,5},{8,10},{9,11},{10,... | collective-permute-start | bytes 294920 | tf_op jit(solution)/shard_map/ppermute | solution.py:86
  154.6 32.2 %collective-permute-start.12 = (bf16[32,1536]{1,0:T(8,128)(2,1)}, bf16[32,1536]{1,0:T(8,128)(2,1)}, u32[]{:S(2)}, u32[]{:S(2)}) collective-permute-start(bf16[32,1536]{1,0:T(8,128)(2,1)} %get-tuple-element.28), channel_id=1, source_target_pairs={{0,1},{1,2},{2,3},{3,0},{4,5},{5,6},{6,7},{7,4},{8,9},{9,10},{10,1... | collective-permute-start | bytes 294920 | tf_op jit(solution)/shard_map/ppermute | solution.py:86
  (7 other events, 49.7 us)
